TPU v7x, 256 devices: a whole 4x4x8 slice. The times are simulated.
256 devices in a mesh: dp: 8 (over x, z_lo), ctx: 32 (over y, z_hi, core).
Axes of the slice: x: 4, y: 4, z: 8 (z_hi: 4, z_lo: 2; z = z_hi * 2 + z_lo), core: 2. Of those that a mesh axis runs over, the one named last changes fastest.
Arguments:
- cont_query: bfloat16 [81920, 1536], P(('dp', 'ctx')), parts along dimension 0, may hold values from -8 to 8
- cont_key: bfloat16 [81920, 1536], P(('dp', 'ctx')), parts along dimension 0, may hold values from -6 to 6
- cont_value: bfloat16 [81920, 1536], P(('dp', 'ctx')), parts along dimension 0, may hold values from -6 to 6
- prompt_key: bfloat16 [65536, 1536], P(('dp', 'ctx')), parts along dimension 0, may hold values from -8 to 8
- prompt_value: bfloat16 [65536, 1536], P(('dp', 'ctx')), parts along dimension 0, may hold values from -6 to 6
- out_grad: bfloat16 [81920, 1536], P(('dp', 'ctx')), parts along dimension 0, may hold values from -6 to 6
- prompt_links: int32 [256, 3], P(('dp', 'ctx')), parts along dimension 0, may hold values from 0 to 1, as said below
- cont_start: int32 [256], P(('dp', 'ctx')), parts along dimension 0, may hold values from 0 to 31, as said below
- valid_len: int32 [256], P('dp'), parts along dimension 0, may hold values from 80 to 320, as said below
Outputs:
- attended: bfloat16 [81920, 1536], P(('dp', 'ctx')), parts along dimension 0
- query_grad: bfloat16 [81920, 1536], P(('dp', 'ctx')), parts along dimension 0
- cont_key_grad: bfloat16 [81920, 1536], P(('dp', 'ctx')), parts along dimension 0
- cont_value_grad: bfloat16 [81920, 1536], P(('dp', 'ctx')), parts along dimension 0
- prompt_key_grad: bfloat16 [65536, 1536], P(('dp', 'ctx')), parts along dimension 0
- prompt_value_grad: bfloat16 [65536, 1536], P(('dp', 'ctx')), parts along dimension 0
There are 8 independent parts, one for each index of `dp`. A program takes and returns all parts, laid end to end along the dimension named above; each array names one. Nothing has to cross between parts.
Inputs may be any that keep to these rules, and one draw needn't show every extreme that they name: `prompt_links`: 1 where continuation block j reads prompt block j - d (column d), else 0; column 0 is always 1; no link points before block 0. `cont_start`: j or j - 1 for block j; a continuation is a run of 1 to 2 consecutive blocks. `valid_len`: 320 in every block but the last of its continuation.
All inputs are finite; a program needn't handle non-finite values.
Results may differ from a plain program's by a relative error of at most 0.0087.
Values may be sent and summed in bfloat16 or wider, within the bound.
A program may use at most 192 MiB of HBM per device.

v0:
```python
import functools

import jax
import jax.numpy as jnp
from jax import lax
from jax.experimental import pallas as pl
from jax.experimental.pallas import tpu as pltpu
from jax.sharding import PartitionSpec as P

HD = 64
PAIR = 2 * HD
QUERY_AHEAD = 3
FAR_AHEAD = 3
SIB_AHEAD = 3
MERGE_LAG = 2
BACK_LAG = 4
LAG = 6
SCALE = HD ** (-0.5)
LOG2E = 1.4426950408889634
F32 = jnp.float32
BF16 = jnp.bfloat16
MESH = pl.DeviceIdType.MESH


def mm(a, b):
    return lax.dot_general(a, b, (((1,), (0,)), ((), ())), preferred_element_type=F32)


def mm_t(a, b):
    return lax.dot_general(a, b, (((1,), (1,)), ((), ())), preferred_element_type=F32)


def stacked(x):
    first = lax.broadcasted_iota(jnp.int32, x.shape, 1) < HD
    zero = jnp.zeros((), x.dtype)
    return jnp.concatenate([jnp.where(first, x, zero), jnp.where(first, zero, x)], 0)


def folded(x):
    half = x.shape[0] // 2
    first = lax.broadcasted_iota(jnp.int32, (half, PAIR), 1) < HD
    return jnp.where(first, x[:half], x[half:])


def as_rows(a, b, c):
    lane = lax.broadcasted_iota(jnp.int32, (a.shape[0], PAIR), 1)
    turned = jnp.where(lane == 0, a, jnp.where(lane == 1, b, c)).T
    return turned[0:1], turned[1:2], turned[2:3]


def spread(row):
    return jnp.broadcast_to(row, (PAIR, row.shape[1])).T


def repeated(x, count):
    return jnp.concatenate([x] * (-(-count // PAIR)), 1)[:, :count]


def softmax_parts(s, v):
    top = jnp.max(s, axis=1, keepdims=True)
    e = jnp.exp2((s - top) * LOG2E)
    total = jnp.sum(e, axis=1, keepdims=True)
    e = e.astype(BF16)
    return top, total, e, mm(e, v)


def row_dot(gs, out):
    return jnp.sum(gs.astype(F32) * out, axis=1, keepdims=True)


def gradients(e, qs, gs, k, v, delta, factor):
    shifted = mm_t(gs, v) - repeated(delta, k.shape[0])
    ds = (e.astype(F32) * shifted).astype(BF16)
    dq = folded(mm(ds, k) * (factor * SCALE))
    dk = mm((qs.astype(F32) * factor).astype(BF16).T, ds).T
    dv = mm((gs.astype(F32) * factor).astype(BF16).T, e).T
    return dq, (dk, dv)


def kernel(
    chunks,
    length,
    q_ref,
    g_ref,
    ck_ref,
    cv_ref,
    pk_ref,
    pv_ref,
    links_ref,
    start_ref,
    valid_ref,
    o_ref,
    dq_ref,
    ckg_ref,
    cvg_ref,
    pkg_ref,
    pvg_ref,
    kv,
    mine,
    theirs,
    bias,
    row_bias,
    their_bias,
    exps,
    sums,
    own,
    own_dq,
    part_o,
    got_o,
    part_s,
    got_s,
    back_s,
    got_back,
    part_dq,
    got_dq,
    sib_g,
    got_sib,
    far_g,
    got_far,
    out_o,
    out_dq,
    out_g,
    kv_in,
    q_in,
    sib_out,
    sib_in,
    far_out,
    far_in,
    qg_out,
    qg_in,
    o_out,
    o_in,
    s_out,
    s_in,
    b_out,
    b_in,
    dq_out,
    dq_in,
    sg_out,
    sg_in,
    fg_out,
    fg_in,
    res_o,
    res_dq,
    res_g,
    rb_out,
    rb_in,
):
    step = pl.program_id(0)
    cb = ck_ref.shape[0]
    pb = pk_ref.shape[0]
    both = cb + pb
    j = lax.axis_index("ctx")
    parity = lax.rem(j, 2)
    even = parity == 0
    odd = parity == 1
    sib = j + 1 - 2 * parity
    nxt = lax.rem(j + 2, length)
    prv = lax.rem(j + length - 2, length)
    has_next = j + 2 < length
    has_prev = j >= 2
    slots = own.shape[0]
    e_slots = exps.shape[0]

    def cols(c):
        return pl.ds(pl.multiple_of(c * PAIR, PAIR), PAIR)

    def send(src, dst, out_sem, in_sem, to):
        pltpu.make_async_remote_copy(
            src_ref=src,
            dst_ref=dst,
            send_sem=out_sem,
            recv_sem=in_sem,
            device_id={"ctx": to},
            device_id_type=MESH,
        ).start()

    def wait_bytes(ref, sem):
        pltpu.make_async_copy(ref, ref, sem).wait()

    def own_rows(c):
        return kv.at[c, :, pl.ds(0, both)]

    def sib_rows(c):
        return kv.at[c, :, pl.ds(both, both)]

    def far_rows(c):
        return kv.at[c, :, pl.ds(2 * both, pb)]

    def send_far(c):
        for which, prompt in enumerate((pk_ref, pv_ref)):
            send(
                prompt.at[:, cols(c)],
                kv.at[c, which, pl.ds(2 * both, pb)],
                far_out.at[c],
                far_in.at[c],
                nxt,
            )

    def send_queries(c):
        send(q_ref.at[:, cols(c)], theirs.at[c, 0], qg_out.at[c], qg_in.at[c], prv)
        send(g_ref.at[:, cols(c)], theirs.at[c, 1], qg_out.at[c], qg_in.at[c], prv)

    def send_sib(c):
        for which, (cont, prompt) in enumerate(((ck_ref, pk_ref), (cv_ref, pv_ref))):
            cont_c, prompt_c = cont.at[:, cols(c)], prompt.at[:, cols(c)]
            send(
                prompt_c, kv.at[c, which, pl.ds(both, pb)], sib_out.at[c], sib_in.at[c], sib
            )
            send(
                cont_c,
                kv.at[c, which, pl.ds(both + pb, cb)],
                sib_out.at[c],
                sib_in.at[c],
                sib,
            )
            pltpu.make_async_copy(cont_c, kv.at[c, which, pl.ds(0, cb)], kv_in.at[c]).start()
            pltpu.make_async_copy(prompt_c, kv.at[c, which, pl.ds(cb, pb)], kv_in.at[c]).start()
        pltpu.make_async_copy(q_ref.at[:, cols(c)], mine.at[c, 0], q_in.at[c]).start()
        pltpu.make_async_copy(g_ref.at[:, cols(c)], mine.at[c, 1], q_in.at[c]).start()

    def rows_of(ref, c, block):
        live = lax.broadcasted_iota(jnp.int32, (cb, 1), 0) < valid_ref[block]
        qs = stacked(ref[c, 0] * jnp.asarray(SCALE, BF16))
        gs = stacked(jnp.where(live, ref[c, 1].astype(F32), 0.0)).astype(BF16)
        return live, qs, gs

    def put_o(c, value):
        out_o[c] = value.astype(BF16)
        pltpu.make_async_copy(out_o.at[c], o_ref.at[:, cols(c)], res_o.at[c]).start()

    def put_dq(c, value):
        out_dq[c] = value.astype(BF16)
        pltpu.make_async_copy(out_dq.at[c], dq_ref.at[:, cols(c)], res_dq.at[c]).start()

    @pl.when(step == 0)
    def _():
        barrier = pltpu.get_barrier_semaphore()

        def greet(other):
            pl.semaphore_signal(barrier, inc=1, device_id={"ctx": other}, device_id_type=MESH)

        greet(sib)

        @pl.when(has_next)
        def _():
            greet(nxt)

        @pl.when(has_prev)
        def _():
            greet(prv)

        @pl.when(has_next & has_prev)
        def _():
            pl.semaphore_wait(barrier, 3)

        @pl.when(jnp.logical_not(has_next & has_prev))
        def _():
            pl.semaphore_wait(barrier, 2)

        @pl.when(jnp.logical_not(has_prev))
        def _():
            got_s[:, 0:1] = jnp.full((chunks, 1, 2 * cb), -1e30, F32)
            got_s[:, 1:2] = jnp.zeros((chunks, 1, 2 * cb), F32)
            got_o[...] = jnp.zeros(got_o.shape, BF16)
            got_dq[...] = jnp.zeros(got_dq.shape, BF16)
            kv[:, :, 2 * both :, :] = jnp.zeros((chunks, 2, pb, PAIR), BF16)

        @pl.when(jnp.logical_not(has_next))
        def _():
            theirs[...] = jnp.zeros(theirs.shape, BF16)
            their_bias[...] = jnp.zeros(their_bias.shape, F32)
            got_back[...] = jnp.zeros(got_back.shape, F32)
            got_far[...] = jnp.zeros(got_far.shape, BF16)


        @pl.when(even & has_prev)
        def _():
            for c in range(QUERY_AHEAD):
                send_queries(c)

        @pl.when(odd & has_next)
        def _():
            for c in range(FAR_AHEAD):
                send_far(c)

        for c in range(SIB_AHEAD):
            send_sib(c)
        near_cont = jnp.where(
            start_ref[0] <= j - 1, valid_ref[jnp.maximum(j - 1, 0)], 0
        )
        own_len = valid_ref[j]
        limits = [jnp.where(links_ref[0, d] > 0, pb, 0) for d in range(3)]
        far_key = lax.broadcasted_iota(jnp.int32, row_bias.shape, 1)
        far_limit = jnp.where(
            far_key < pb,
            limits[2],
            jnp.where(far_key < 2 * pb, limits[1] + pb, near_cont + 2 * pb),
        )
        row_bias[...] = jnp.where(far_key < far_limit, 0.0, -1e30)

        @pl.when(even & has_prev)
        def _():
            send(row_bias, their_bias, rb_out, rb_in, prv)

        key = lax.broadcasted_iota(jnp.int32, (cb, 2 * both + pb), 1)
        query = lax.broadcasted_iota(jnp.int32, (cb, 2 * both + pb), 0)
        limit = jnp.where(
            key < cb,
            jnp.minimum(query, own_len - 1) + 1,
            jnp.where(
                key < both,
                limits[0] + cb,
                jnp.where(
                    key < both + pb,
                    limits[1] + both,
                    jnp.where(
                        key < 2 * both, near_cont + (both + pb), limits[2] + 2 * both
                    ),
                ),
            ),
        )
        bias[...] = jnp.where(key < limit, 0.0, -1e30)

        @pl.when(even & has_next)
        def _():
            wait_bytes(their_bias, rb_in)

    @pl.when((step > 0) & (step + SIB_AHEAD <= chunks))
    def _():
        send_sib(step + SIB_AHEAD - 1)

    @pl.when((step > 0) & (step + QUERY_AHEAD <= chunks) & even & has_prev)
    def _():
        send_queries(step + QUERY_AHEAD - 1)

    @pl.when((step > 0) & (step + FAR_AHEAD <= chunks) & odd & has_next)
    def _():
        send_far(step + FAR_AHEAD - 1)

    @pl.when((step < chunks) & odd)
    def _():
        c = step
        wait_bytes(own_rows(c), kv_in.at[c])
        wait_bytes(mine.at[c], q_in.at[c])
        wait_bytes(sib_rows(c), sib_in.at[c])

        @pl.when(has_prev)
        def _():
            wait_bytes(far_rows(c), far_in.at[c])

        live, qs, gs = rows_of(mine, c, j)
        k = kv[c, 0]
        v = kv[c, 1]
        b = bias[...]
        s = mm_t(qs, k) + jnp.concatenate([b, b], 0)
        top, total, e, out = softmax_parts(s, v)
        inverse = jnp.broadcast_to(1.0 / total, out.shape)
        out = out * inverse
        put_o(c, jnp.where(live, folded(out), 0.0))
        delta = jnp.broadcast_to(row_dot(gs, out), out.shape)
        dq, grads = gradients(e, qs, gs, k, v, delta, inverse)
        put_dq(c, dq)
        for which in range(2):
            own[lax.rem(c, slots), which] = grads[which][:both]
            sib_g[c, which] = grads[which][both : 2 * both].astype(BF16)
            far_g[c, which] = grads[which][2 * both :].astype(BF16)

        @pl.when(has_prev)
        def _():
            send(far_g.at[c], got_far.at[c], fg_out.at[c], fg_in.at[c], prv)

        send(sib_g.at[c], got_sib.at[c], sg_out.at[c], sg_in.at[c], sib)

    def wait_first(c):
        wait_bytes(own_rows(c), kv_in.at[c])
        wait_bytes(mine.at[c], q_in.at[c])
        wait_bytes(sib_rows(c), sib_in.at[c])

        @pl.when(has_next)
        def _():
            wait_bytes(theirs.at[c], qg_in.at[c])

    def wait_merge(c):
        @pl.when(has_prev)
        def _():
            wait_bytes(got_s.at[c], s_in.at[c])
            wait_bytes(got_o.at[c], o_in.at[c])

    def wait_back(c):
        @pl.when(has_next)
        def _():
            wait_bytes(got_back.at[c], b_in.at[c])

    def first(c):
        slot = lax.rem(c, e_slots)
        _, qs, gs = rows_of(theirs, c, nxt)
        k = kv[c, 0, cb : 2 * both]
        v = kv[c, 1, cb : 2 * both]
        s = mm_t(qs, k) + their_bias[0:1, :]
        top, total, e, out = softmax_parts(s, v)
        part_o[c] = folded(out * (1.0 / total)).astype(BF16)
        top, total, delta = as_rows(top, total, row_dot(gs, out))
        part_s[c, 0:1] = (top + jnp.log(total)) * LOG2E
        part_s[c, 1:2] = delta / total
        exps[slot] = e
        sums[slot, 0:1] = total

    def merge(c):
        slot = lax.rem(c, slots)
        live, qs, gs = rows_of(mine, c, j)
        k = kv[c, 0, :both]
        v = kv[c, 1, :both]
        b = bias[:, :both]
        s = mm_t(qs, k) + jnp.concatenate([b, b], 0)
        top, total, e, out = softmax_parts(s, v)
        top, total, delta = as_rows(top, total, row_dot(gs, out))
        level = (top + jnp.log(total)) * LOG2E
        far_level = got_s[c, 0:1]
        high = jnp.maximum(level, far_level)
        mix = high + jnp.log(jnp.exp2(level - high) + jnp.exp2(far_level - high)) * LOG2E
        factor = jnp.exp2(level - mix) / total
        far_share = jnp.exp2(far_level - mix)
        delta = factor * delta + far_share * got_s[c, 1:2]
        back_s[c, 0:1] = far_share
        back_s[c, 1:2] = delta
        factor = spread(factor)
        mixed = folded(out * factor) + folded(spread(far_share)) * got_o[c].astype(F32)
        out_o[c] = jnp.where(live, mixed, 0.0).astype(BF16)
        dq, grads = gradients(e, qs, gs, k, v, spread(delta), factor)
        own_dq[slot] = dq
        for which in range(2):
            own[slot, which] = grads[which]

    def back(c):
        slot = lax.rem(c, e_slots)
        _, qs, gs = rows_of(theirs, c, nxt)
        k = kv[c, 0, cb : 2 * both]
        v = kv[c, 1, cb : 2 * both]
        factor = spread(got_back[c, 0:1] / sums[slot, 0:1])
        delta = spread(got_back[c, 1:2])
        dq, grads = gradients(exps[slot], qs, gs, k, v, delta, factor)
        part_dq[c] = dq.astype(BF16)
        for which in range(2):
            own[lax.rem(c, slots), which, cb:, :] += grads[which][:pb]
            sib_g[c, which] = grads[which][pb:].astype(BF16)

    def send_first(c):
        @pl.when(has_next)
        def _():
            send(part_s.at[c], got_s.at[c], s_out.at[c], s_in.at[c], nxt)
            send(part_o.at[c], got_o.at[c], o_out.at[c], o_in.at[c], nxt)

    def send_merge(c):
        @pl.when(has_prev)
        def _():
            send(back_s.at[c], got_back.at[c], b_out.at[c], b_in.at[c], prv)

        pltpu.make_async_copy(out_o.at[c], o_ref.at[:, cols(c)], res_o.at[c]).start()

    def send_back(c):
        @pl.when(has_next)
        def _():
            send(part_dq.at[c], got_dq.at[c], dq_out.at[c], dq_in.at[c], nxt)

        send(sib_g.at[c], got_sib.at[c], sg_out.at[c], sg_in.at[c], sib)

    at_merge = step - MERGE_LAG
    at_back = step - BACK_LAG
    steady = (at_back >= 0) & (step < chunks)

    @pl.when(steady & even)
    def _():
        wait_back(at_back)
        wait_merge(at_merge)
        wait_first(step)
        merge(at_merge)
        back(at_back)
        first(step)
        send_merge(at_merge)
        send_first(step)
        send_back(at_back)

    @pl.when((step < BACK_LAG) & even)
    def _():
        wait_first(step)
        first(step)
        send_first(step)

    @pl.when((at_merge >= 0) & (at_merge < chunks) & even & jnp.logical_not(steady))
    def _():
        wait_merge(at_merge)
        merge(at_merge)
        send_merge(at_merge)

    @pl.when((step >= chunks) & (at_back < chunks) & even)
    def _():
        wait_back(at_back)
        back(at_back)
        send_back(at_back)

    @pl.when(step >= LAG)
    def _():
        c = step - LAG
        slot = lax.rem(c, slots)

        @pl.when(odd)
        def _():
            @pl.when(has_next)
            def _():
                wait_bytes(got_far.at[c], fg_in.at[c])

            own[slot, :, cb:, :] += got_far[c].astype(F32)

        @pl.when(even)
        def _():
            @pl.when(has_prev)
            def _():
                wait_bytes(got_dq.at[c], dq_in.at[c])

            put_dq(c, own_dq[slot] + got_dq[c].astype(F32))

        wait_bytes(got_sib.at[c], sg_in.at[c])
        for which, (cont, prompt) in enumerate(((ckg_ref, pkg_ref), (cvg_ref, pvg_ref))):
            out_g[c, which, :cb, :] = (
                own[slot, which, :cb, :] + got_sib[c, which, pb:, :].astype(F32)
            ).astype(BF16)
            out_g[c, which, cb:, :] = (
                own[slot, which, cb:, :] + got_sib[c, which, :pb, :].astype(F32)
            ).astype(BF16)
            pltpu.make_async_copy(
                out_g.at[c, which, pl.ds(0, cb)], cont.at[:, cols(c)], res_g.at[c]
            ).start()
            pltpu.make_async_copy(
                out_g.at[c, which, pl.ds(cb, pb)], prompt.at[:, cols(c)], res_g.at[c]
            ).start()

    @pl.when(step == chunks + LAG - 1)
    def _():
        def finish(c, carry):
            wait_bytes(sib_rows(c), sib_out.at[c])
            wait_bytes(sib_g.at[c], sg_out.at[c])
            wait_bytes(out_o.at[c], res_o.at[c])
            wait_bytes(out_dq.at[c], res_dq.at[c])
            wait_bytes(out_g.at[c], res_g.at[c])

            @pl.when(even & has_prev)
            def _():
                wait_bytes(theirs.at[c], qg_out.at[c])
                wait_bytes(back_s.at[c], b_out.at[c])

            @pl.when(even & has_next)
            def _():
                wait_bytes(part_o.at[c], o_out.at[c])
                wait_bytes(part_s.at[c], s_out.at[c])
                wait_bytes(part_dq.at[c], dq_out.at[c])

            @pl.when(odd & has_next)
            def _():
                wait_bytes(far_rows(c), far_out.at[c])

            @pl.when(odd & has_prev)
            def _():
                wait_bytes(far_g.at[c], fg_out.at[c])

            return carry

        lax.fori_loop(0, chunks, finish, 0)

        @pl.when(even & has_prev)
        def _():
            wait_bytes(row_bias, rb_out)


def hand_over(*refs):
    count = (len(refs) - 2) // 3
    sources, targets, held = refs[:count], refs[count : 2 * count], refs[2 * count : 3 * count]
    sems_in, sems_out = refs[-2:]
    loads = [
        pltpu.make_async_copy(sources[i], held[i], sems_in.at[i]) for i in range(count)
    ]
    stores = [
        pltpu.make_async_copy(held[i], targets[i], sems_out.at[i]) for i in range(count)
    ]
    for load in loads:
        load.start()
    for load, store in zip(loads, stores):
        load.wait()
        store.start()
    for store in stores:
        store.wait()


def per_device(*args):
    q, ck, cv, pk, pv, g, links, start, valid = args
    cb, width = q.shape
    pb = pk.shape[0]
    chunks = width // PAIR
    length = lax.axis_size("ctx")
    keys = 2 * cb + 3 * pb
    both = cb + pb
    far_keys = cb + 2 * pb
    anywhere = pl.BlockSpec(memory_space=pl.ANY)
    scalars = pl.BlockSpec(memory_space=pltpu.SMEM)
    wide = jax.ShapeDtypeStruct((cb, width), BF16)
    short = jax.ShapeDtypeStruct((pb, width), BF16)
    work = 12 * cb * keys * width
    rows = pltpu.VMEM((chunks, cb, PAIR), BF16)
    stats = pltpu.VMEM((chunks, 2, 2 * cb), F32)
    pair_rows = pltpu.VMEM((chunks, 2, cb, PAIR), BF16)
    sib_grad = pltpu.VMEM((chunks, 2, both, PAIR), BF16)
    far_grad = pltpu.VMEM((chunks, 2, pb, PAIR), BF16)
    results = pl.pallas_call(
        functools.partial(kernel, chunks, length),
        grid=(chunks + LAG,),
        in_specs=[anywhere] * 6 + [scalars] * 3,
        out_specs=[anywhere] * 6,
        out_shape=[wide, wide, wide, wide, short, short],
        scratch_shapes=[
            pltpu.VMEM((chunks, 2, keys, PAIR), BF16),
            pair_rows,
            pair_rows,
            pltpu.VMEM((cb, keys), F32),
            pltpu.VMEM((8, far_keys), F32),
            pltpu.VMEM((8, far_keys), F32),
            pltpu.VMEM((BACK_LAG + 1, 2 * cb, far_keys), BF16),
            pltpu.VMEM((BACK_LAG + 1, 2, 2 * cb), F32),
            pltpu.VMEM((LAG + 1, 2, both, PAIR), F32),
            pltpu.VMEM((LAG + 1, cb, PAIR), F32),
            rows,
            rows,
            stats,
            stats,
            stats,
            stats,
            rows,
            rows,
            sib_grad,
            sib_grad,
            far_grad,
            far_grad,
            rows,
            rows,
            sib_grad,
        ]
        + [pltpu.SemaphoreType.DMA((chunks,))] * 23
        + [pltpu.SemaphoreType.DMA] * 2,
        compiler_params=pltpu.CompilerParams(
            collective_id=0, has_side_effects=True, vmem_limit_bytes=60 * 2**20
        ),
        cost_estimate=pl.CostEstimate(
            flops=work, bytes_accessed=12 * 2 * cb * width, transcendentals=cb * keys * width // HD
        ),
        name="pairs",
    )(q, g, ck, cv, pk, pv, links, start, valid)
    return pl.pallas_call(
        hand_over,
        in_specs=[anywhere] * 6,
        out_specs=[anywhere] * 6,
        out_shape=[wide, wide, wide, wide, short, short],
        scratch_shapes=[pltpu.VMEM(shape.shape, BF16) for shape in (wide,) * 4 + (short,) * 2]
        + [pltpu.SemaphoreType.DMA((6,))] * 2,
        name="hand_over",
    )(*results)


def solution(mesh):
    rows = P(("dp", "ctx"), None)
    return jax.shard_map(
        per_device,
        mesh=mesh,
        in_specs=(rows,) * 7 + (P(("dp", "ctx")), P("dp")),
        out_specs=(rows,) * 6,
        check_vma=False,
    )
```

profile of v0, /device:TPU:12, one launch (start us, length us, event | category | flops | bytes accessed | tf_op | source)
XLA Modules:
  0.0 126.7 jit_solution(6768896161433268058)
XLA Ops:
  1.3 120.8 %pairs.1 = (bf16[320,1536]{1,0:T(8,128)(2,1)}, bf16[320,1536]{1,0:T(8,128)(2,1)}, bf16[320,1536]{1,0:T(8,128)(2,1)}, bf16[320,1536]{1,0:T(8,128)(2,1)}, bf16[256...) custom-call(bf16[320,1536]{1,0:T(8,128)(2,1)} %q_ref.1, bf16[320,1536]{1,0:T(8,128)(2,1)} %g_ref.1, ...), custom_call_target="tpu_custom_call" | custom-call | flops 8304721920 | bytes 11796480 | tf_op jit(solution)/shard_map/pairs/pallas_call | solution.py:613
  122.1 4.6 %hand_over.1 = (bf16[320,1536]{1,0:T(8,128)(2,1)}, bf16[320,1536]{1,0:T(8,128)(2,1)}, bf16[320,1536]{1,0:T(8,128)(2,1)}, bf16[320,1536]{1,0:T(8,128)(2,1)}, bf16...) custom-call(bf16[320,1536]{1,0:T(8,128)(2,1)} %get-tuple-element.12.refs_0_, ...), custom_call_target="tpu_custom_call" | custom-call | tf_op jit(solution)/shard_map/hand_over/pallas_call | solution.py:656
where the time goes:
time: 127 us
  Pallas kernels  125 us (98%)
  between operations  1.29 us (1%)
    pallas_call x1, Pallas kernels, per_device(): pl.pallas_call(functools.partial(kernel, chunks, length), grid=(chunks +...  121 us
    pallas_call x1, Pallas kernels, per_device(): pl.pallas_call(hand_over, in_specs=[anywhere] * 6, out_specs=[anywhere] *...  4.63 us

commit v1 on v0

--- a/solution.py
+++ b/solution.py
@@ -10,11 +10,12 @@
 HD = 64
 PAIR = 2 * HD
 QUERY_AHEAD = 3
-FAR_AHEAD = 3
+FAR_AHEAD = 4
 SIB_AHEAD = 3
 MERGE_LAG = 2
+RETURN_LAG = 4
 BACK_LAG = 4
-LAG = 6
+LAG = 7
 SCALE = HD ** (-0.5)
 LOG2E = 1.4426950408889634
 F32 = jnp.float32
@@ -338,6 +339,11 @@
     def _():
         send_far(step + FAR_AHEAD - 1)
 
+    @pl.when((step >= RETURN_LAG) & (step < chunks + RETURN_LAG) & odd & has_prev)
+    def _():
+        c = step - RETURN_LAG
+        send(far_g.at[c], got_far.at[c], fg_out.at[c], fg_in.at[c], prv)
+
     @pl.when((step < chunks) & odd)
     def _():
         c = step
@@ -365,11 +371,6 @@
             own[lax.rem(c, slots), which] = grads[which][:both]
             sib_g[c, which] = grads[which][both : 2 * both].astype(BF16)
             far_g[c, which] = grads[which][2 * both :].astype(BF16)
-
-        @pl.when(has_prev)
-        def _():
-            send(far_g.at[c], got_far.at[c], fg_out.at[c], fg_in.at[c], prv)
-
         send(sib_g.at[c], got_sib.at[c], sg_out.at[c], sg_in.at[c], sib)
 
     def wait_first(c):

time: 127 us -> 121 us (0.953)
  Pallas kernels: 125 us -> 119 us
    pallas_call x1, Pallas kernels: 121 us -> 115 us  [per_device(): pl.pallas_call(functools.partial(kernel, chunks, length), grid=(chunks +...]
where the time goes in v1:
time: 121 us
  Pallas kernels  119 us (98%)
  between operations  1.29 us (1%)
    pallas_call x1, Pallas kernels, per_device(): pl.pallas_call(functools.partial(kernel, chunks, length), grid=(chunks +...  115 us
    pallas_call x1, Pallas kernels, per_device(): pl.pallas_call(hand_over, in_specs=[anywhere] * 6, out_specs=[anywhere] *...  4.63 us

profile of v1, /device:TPU:12, one launch (start us, length us, event | category | flops | bytes accessed | tf_op | source)
XLA Modules:
  0.0 120.6 jit_solution(11227097493855323426)
XLA Ops:
  1.3 114.7 %pairs.1 = (bf16[320,1536]{1,0:T(8,128)(2,1)}, bf16[320,1536]{1,0:T(8,128)(2,1)}, bf16[320,1536]{1,0:T(8,128)(2,1)}, bf16[320,1536]{1,0:T(8,128)(2,1)}, bf16[256...) custom-call(bf16[320,1536]{1,0:T(8,128)(2,1)} %q_ref.1, bf16[320,1536]{1,0:T(8,128)(2,1)} %g_ref.1, ...), custom_call_target="tpu_custom_call" | custom-call | flops 8304721920 | bytes 11796480 | tf_op jit(solution)/shard_map/pairs/pallas_call | solution.py:614
  116.0 4.6 %hand_over.1 = (bf16[320,1536]{1,0:T(8,128)(2,1)}, bf16[320,1536]{1,0:T(8,128)(2,1)}, bf16[320,1536]{1,0:T(8,128)(2,1)}, bf16[320,1536]{1,0:T(8,128)(2,1)}, bf16...) custom-call(bf16[320,1536]{1,0:T(8,128)(2,1)} %get-tuple-element.12.refs_0_, ...), custom_call_target="tpu_custom_call" | custom-call | tf_op jit(solution)/shard_map/hand_over/pallas_call | solution.py:657

commit v2 on v1

--- a/solution.py
+++ b/solution.py
@@ -468,7 +468,7 @@
 
     at_merge = step - MERGE_LAG
     at_back = step - BACK_LAG
-    steady = (at_back >= 0) & (step < chunks)
+    steady = (at_back >= 0) & (step < chunks - 1)
 
     @pl.when(steady & even)
     def _():
@@ -494,11 +494,17 @@
         merge(at_merge)
         send_merge(at_merge)
 
-    @pl.when((step >= chunks) & (at_back < chunks) & even)
+    @pl.when((step >= chunks - 1) & (at_back < chunks) & even)
     def _():
         wait_back(at_back)
         back(at_back)
         send_back(at_back)
+
+    @pl.when((step == chunks - 1) & even)
+    def _():
+        wait_first(step)
+        first(step)
+        send_first(step)
 
     @pl.when(step >= LAG)
     def _():

time: 121 us -> 122 us (level)
  Pallas kernels: 119 us -> 121 us
    pallas_call x1, Pallas kernels: 115 us -> 116 us  [per_device(): pl.pallas_call(functools.partial(kernel, chunks, length), grid=(chunks +...]
where the time goes in v2:
time: 122 us
  Pallas kernels  121 us (99%)
  between operations  1.29 us (1%)
    pallas_call x1, Pallas kernels, per_device(): pl.pallas_call(functools.partial(kernel, chunks, length), grid=(chunks +...  116 us
    pallas_call x1, Pallas kernels, per_device(): pl.pallas_call(hand_over, in_specs=[anywhere] * 6, out_specs=[anywhere] *...  4.63 us

profile of v2, /device:TPU:12, one launch (start us, length us, event | category | flops | bytes accessed | tf_op | source)
XLA Modules:
  0.0 122.1 jit_solution(1606690641663265699)
XLA Ops:
  1.3 116.1 %pairs.1 = (bf16[320,1536]{1,0:T(8,128)(2,1)}, bf16[320,1536]{1,0:T(8,128)(2,1)}, bf16[320,1536]{1,0:T(8,128)(2,1)}, bf16[320,1536]{1,0:T(8,128)(2,1)}, bf16[256...) custom-call(bf16[320,1536]{1,0:T(8,128)(2,1)} %q_ref.1, bf16[320,1536]{1,0:T(8,128)(2,1)} %g_ref.1, ...), custom_call_target="tpu_custom_call" | custom-call | flops 8304721920 | bytes 11796480 | tf_op jit(solution)/shard_map/pairs/pallas_call | solution.py:620
  117.4 4.6 %hand_over.1 = (bf16[320,1536]{1,0:T(8,128)(2,1)}, bf16[320,1536]{1,0:T(8,128)(2,1)}, bf16[320,1536]{1,0:T(8,128)(2,1)}, bf16[320,1536]{1,0:T(8,128)(2,1)}, bf16...) custom-call(bf16[320,1536]{1,0:T(8,128)(2,1)} %get-tuple-element.12.refs_0_, ...), custom_call_target="tpu_custom_call" | custom-call | tf_op jit(solution)/shard_map/hand_over/pallas_call | solution.py:663
